TPU v7x, 32 devices: a whole 2x2x4 slice. The times are simulated.
32 devices in a mesh: tm: 8 (over z, x), chan: 4 (over y, core).
Axes of the slice: x: 2, y: 2, z: 4, core: 2. Of those that a mesh axis runs over, the one named last changes fastest.
Arguments:
- visibilities: bfloat16 [2, 4096, 16, 2048], P(None, 'tm', 'chan'), may hold values from -24 to 24
- beam_transfer: bfloat16 [2, 16, 2048, 256], P(None, 'chan'), may hold values from -0.125 to 0.125
- sky_modes: bfloat16 [2, 4096, 16, 256], P(None, 'tm', 'chan'), may hold values from -6 to 6
- inverse_gains: float32 [2, 1024], replicated, may hold values from -6 to 6
- phase_rate: float32 [2048], replicated, may hold values from -0.05 to 0.05
- feed_pairs: int32 [2, 2048], replicated, may hold values from 0 to 1023, as said below
- block_owner: int32 [8], replicated, may hold values from 0 to 7, each once
Outputs:
- sky_grad: bfloat16 [2, 4096, 16, 256], P(None, 'tm', 'chan')
- feed_grad: float32 [2, 1024], P(None, 'tm')
Inputs may be any that keep to these rules, and one draw needn't show every extreme that they name: The two feeds of a baseline differ; every feed appears in feed_pairs[0]. `block_owner`: each device index appears exactly once.
All inputs are finite; a program needn't handle non-finite values.
Results may differ from a plain program's by a relative error of at most 0.0057.
Values may be sent and summed in bfloat16 or wider, within the bound.
A program may use at most 256 MiB of HBM per device.

v0:
```python
import math

import jax
import jax.numpy as jnp
from jax import lax
from jax.sharding import PartitionSpec as P

TIMES = 4096
CH = 16


def turn_table(left_size, right_size, period):
    left_index = lax.broadcasted_iota(jnp.int32, (left_size, right_size), 0)
    right_index = lax.broadcasted_iota(jnp.int32, (left_size, right_size), 1)
    turn_angle = (left_index * right_index % period).astype(jnp.float32) * (2.0 * math.pi / period)
    return (jnp.cos(turn_angle), jnp.sin(turn_angle))


def table_product(pattern, table, operand):
    return jnp.einsum(
        pattern, table, operand, precision=lax.Precision.HIGH, preferred_element_type=jnp.float32
    )


def plain_product(pattern, left_side, right_side):
    return jnp.einsum(pattern, left_side, right_side, preferred_element_type=jnp.float32)


def forward_transform(series):
    all_times = series.shape[1]
    columns = series.shape[2]
    outer_size = math.gcd(all_times, 64)
    inner_size = all_times // outer_size
    shaped = series.reshape(2, outer_size, inner_size, columns)
    cos_one, sin_one = turn_table(outer_size, outer_size, outer_size)
    section_real = table_product("ka,acz->kcz", cos_one, shaped[0]) + table_product(
        "ka,acz->kcz", sin_one, shaped[1]
    )
    section_imag = table_product("ka,acz->kcz", cos_one, shaped[1]) - table_product(
        "ka,acz->kcz", sin_one, shaped[0]
    )
    cos_two, sin_two = turn_table(outer_size, inner_size, all_times)
    twist_real = section_real * cos_two[:, :, None] + section_imag * sin_two[:, :, None]
    twist_imag = section_imag * cos_two[:, :, None] - section_real * sin_two[:, :, None]
    cos_three, sin_three = turn_table(inner_size, inner_size, inner_size)
    final_real = table_product("lc,kcz->lkz", cos_three, twist_real) + table_product(
        "lc,kcz->lkz", sin_three, twist_imag
    )
    final_imag = table_product("lc,kcz->lkz", cos_three, twist_imag) - table_product(
        "lc,kcz->lkz", sin_three, twist_real
    )
    unit_scale = 1.0 / jnp.sqrt(jnp.float32(all_times))
    return jnp.stack([final_real, final_imag]).reshape(2, all_times, columns) * unit_scale


def ordered_spectrum(moved, inverse, devices_tm):
    all_times = moved.shape[1]
    channels = moved.shape[2]
    slab_width = moved.shape[3]
    block_rows = all_times // devices_tm
    series = moved.astype(jnp.float32).reshape(2, all_times, channels * slab_width)
    spectrum = (
        forward_transform(series).reshape(2, all_times, channels, slab_width).astype(jnp.bfloat16)
    )
    ordered = jnp.take(
        spectrum.reshape(2, devices_tm, block_rows, channels, slab_width), inverse, axis=1
    )
    return ordered.reshape(2, all_times, channels, slab_width)


def rotate_back(spectrum, order_values, rates):
    turn_angle = order_values[:, None] * rates[None, :]
    cosine_part = jnp.cos(turn_angle)[:, None, :]
    sine_part = jnp.sin(turn_angle)[:, None, :]
    return (
        cosine_part * spectrum[0] + sine_part * spectrum[1],
        cosine_part * spectrum[1] - sine_part * spectrum[0],
    )


def correlate(filtered_real, filtered_imag, rotated_real, rotated_imag):
    cross_real = jnp.sum(filtered_real * rotated_real + filtered_imag * rotated_imag, axis=(0, 1))
    cross_imag = jnp.sum(filtered_real * rotated_imag - filtered_imag * rotated_real, axis=(0, 1))
    return (cross_real, cross_imag)


def feed_terms(cross_real, cross_imag, feed_first, feed_second, inverse_gains):
    first_gain = inverse_gains[:, feed_first]
    second_gain = inverse_gains[:, feed_second]
    second_real = first_gain[0] * cross_real - first_gain[1] * cross_imag
    second_imag = first_gain[0] * cross_imag + first_gain[1] * cross_real
    first_real = second_gain[0] * cross_real + second_gain[1] * cross_imag
    first_imag = second_gain[1] * cross_real - second_gain[0] * cross_imag
    feed_count = inverse_gains.shape[1]
    summed_real = jax.ops.segment_sum(second_real, feed_second, feed_count) + jax.ops.segment_sum(
        first_real, feed_first, feed_count
    )
    summed_imag = jax.ops.segment_sum(second_imag, feed_second, feed_count) + jax.ops.segment_sum(
        first_imag, feed_first, feed_count
    )
    return jnp.stack([summed_real, summed_imag])


def body(
    visibilities, beam_transfer, sky_modes, inverse_gains, phase_rate, feed_pairs, block_owner
):
    devices_tm = lax.axis_size("tm")
    position = lax.axis_index("tm")
    slab_rows = visibilities.shape[1]
    all_times = slab_rows * devices_tm
    block_rows = all_times // devices_tm
    indices = jnp.arange(devices_tm, dtype=jnp.int32)
    inverse = jnp.sum(
        jnp.where(block_owner[None, :] == indices[:, None], indices[None, :], 0), axis=1
    )
    order_all = (
        inverse[:, None] * block_rows + jnp.arange(block_rows, dtype=jnp.int32)[None, :]
    ).reshape(all_times)
    time_moved = lax.all_to_all(visibilities, "tm", split_axis=3, concat_axis=1, tiled=True)
    ordered = ordered_spectrum(time_moved, inverse, devices_tm)
    received = lax.all_to_all(ordered, "tm", split_axis=1, concat_axis=3, tiled=True)
    own_order = lax.dynamic_slice_in_dim(order_all, position * block_rows, block_rows).astype(
        jnp.float32
    )
    rotated_real, rotated_imag = rotate_back(received.astype(jnp.float32), own_order, phase_rate)
    first_gain = inverse_gains[:, feed_pairs[0]]
    second_gain = inverse_gains[:, feed_pairs[1]]
    pair_real = first_gain[0] * second_gain[0] + first_gain[1] * second_gain[1]
    pair_imag = first_gain[1] * second_gain[0] - first_gain[0] * second_gain[1]
    beam_real = beam_transfer[0]
    beam_imag = beam_transfer[1]
    model_real = plain_product("mfk,fbk->mfb", sky_modes[0], beam_real) - plain_product(
        "mfk,fbk->mfb", sky_modes[1], beam_imag
    )
    model_imag = plain_product("mfk,fbk->mfb", sky_modes[0], beam_imag) + plain_product(
        "mfk,fbk->mfb", sky_modes[1], beam_real
    )
    misfit_real = (pair_real * rotated_real - pair_imag * rotated_imag - model_real).astype(
        jnp.bfloat16
    )
    misfit_imag = (pair_real * rotated_imag + pair_imag * rotated_real - model_imag).astype(
        jnp.bfloat16
    )
    grad_real = (
        plain_product("mfb,fbk->mfk", misfit_real, beam_real)
        + plain_product("mfb,fbk->mfk", misfit_imag, beam_imag)
    ).astype(jnp.bfloat16)
    grad_imag = (
        plain_product("mfb,fbk->mfk", misfit_imag, beam_real)
        - plain_product("mfb,fbk->mfk", misfit_real, beam_imag)
    ).astype(jnp.bfloat16)
    sky_grad = jnp.stack([grad_real, grad_imag])
    filtered_real = plain_product("mfk,fbk->mfb", grad_real, beam_real) - plain_product(
        "mfk,fbk->mfb", grad_imag, beam_imag
    )
    filtered_imag = plain_product("mfk,fbk->mfb", grad_real, beam_imag) + plain_product(
        "mfk,fbk->mfb", grad_imag, beam_real
    )
    cross_real, cross_imag = correlate(filtered_real, filtered_imag, rotated_real, rotated_imag)
    partial_grad = feed_terms(cross_real, cross_imag, feed_pairs[0], feed_pairs[1], inverse_gains)
    feed_share = lax.psum_scatter(partial_grad, "tm", scatter_dimension=1, tiled=True)
    summed = lax.psum(feed_share, "chan")
    grad_scale = 0.25 / (TIMES * CH)
    return (sky_grad, summed * grad_scale)


def solution(mesh):
    placed = (
        P(None, "tm", "chan", None),
        P(None, "chan", None, None),
        P(None, "tm", "chan", None),
        P(),
        P(),
        P(),
        P(),
    )
    return jax.shard_map(
        body,
        mesh=mesh,
        in_specs=placed,
        out_specs=(P(None, "tm", "chan", None), P(None, "tm")),
        check_vma=False,
    )
```

profile of v0, /device:TPU:0, one launch (start us, length us, event | category | flops | bytes accessed | tf_op | source)
XLA Modules:
  0.0 1641.9 jit_solution(2005103043917548032)
XLA Ops:
  7.2 37.2 %copy.159 = bf16[2,512,4,2048]{1,2,0,3:T(4,128)(2,1)} copy(bf16[2,512,4,2048]{3,2,1,0:T(4,128)(2,1)} %param.7) | data formatting | bytes 33554432 | tf_op args[0]
  44.4 7.4 all-to-all-start
  53.7 361.2 %all-to-all-done = bf16[2,512,4,2048]{1,2,0,3:T(4,128)(2,1)} async-done(((bf16[2,512,4,2048]{1,2,0,3:T(4,128)(2,1)}), bf16[2,512,4,2048]{1,2,0,3:T(4,128)(2,1)}, u32[]{:S(2)}, u32[]{:S(2)}) %all-to-all-start) | async-done | bytes 16777248 | tf_op jit(solution)/shard_map/all_to_all | solution.py:119
  414.8 37.5 %copy.160 = bf16[2,512,4,8,256]{4,2,1,3,0:T(4,128)(2,1)} copy(bf16[2,512,4,8,256]{1,2,0,4,3:T(4,128)(2,1)} %bitcast.7) | data formatting | bytes 33554432 | tf_op jit(solution)/shard_map/all_to_all | solution.py:119
  452.3 15.6 fusion.143
  468.0 14.4 squeeze.68
  482.4 23.0 %fusion.25 = f32[64,64,1024]{2,0,1:T(8,128)} fusion(bf16[64,64,1024]{2,1,0:T(8,128)(2,1)} %squeeze.68), kind=kOutput, calls=%fused_computation.45 | convolution fusion | flops 1610670080 | bytes 25165824 | tf_op jit(solution)/shard_map/ka,acz->kcz/dot_general | solution.py:20
  505.5 14.3 squeeze.69
  519.8 22.8 %fusion.21 = f32[64,64,1024]{2,0,1:T(8,128)} fusion(bf16[64,64,1024]{2,1,0:T(8,128)(2,1)} %squeeze.69), kind=kOutput, calls=%fused_computation.41 | convolution fusion | flops 1610670080 | bytes 25165824 | tf_op jit(solution)/shard_map/ka,acz->kcz/dot_general | solution.py:20
  542.5 27.7 %convolution_add_fusion = f32[64,64,1024]{2,0,1:T(8,128)} fusion(f32[64,64,1024]{2,0,1:T(8,128)} %fusion.25, bf16[64,64,1024]{2,1,0:T(8,128)(2,1)} %squeeze.69), kind=kOutput, calls=%fused_computation.40 | convolution fusion | flops 1614864384 | bytes 41943040 | tf_op jit(solution)/shard_map/ka,acz->kcz/dot_general | solution.py:20
  570.2 52.6 %multiply_add_fusion.1 = (f32[64,64,1024]{2,0,1:T(8,128)}, f32[64,64,1024]{2,0,1:T(8,128)}) fusion(f32[64,64,1024]{2,0,1:T(8,128)} %convolution_add_fusion, f32[64,64]{0,1:T(8,128)S(1)} %copy.166, f32[64,64]{0,1:T(8,128)S(1)} %copy.163, f32[64,64,1024]{2,0,1:T(8,128)} %fusion.21, bf16[64,64,1024]{2,1,0:T(8,128)(2,1)} %squeeze.68), kind=kOutput, calls=%fused_computation.28 | convolution fusion | flops 1640030208 | bytes 75530240 | tf_op jit(solution)/shard_map/ka,acz->kcz/dot_general | solution.py:20
  622.8 26.3 %fusion.9 = f32[64,64,1024]{2,0,1:T(8,128)} fusion(f32[64,64,1024]{2,0,1:T(8,128)} %get-tuple-element.23), kind=kOutput, calls=%fused_computation.31 | convolution fusion | flops 1610670080 | bytes 33554432 | tf_op jit(solution)/shard_map/lc,kcz->lkz/dot_general | solution.py:20
  649.2 26.2 %fusion.7 = f32[64,64,1024]{2,0,1:T(8,128)} fusion(f32[64,64,1024]{2,0,1:T(8,128)} %get-tuple-element.23), kind=kOutput, calls=%fused_computation.29 | convolution fusion | flops 1610670080 | bytes 33554432 | tf_op jit(solution)/shard_map/lc,kcz->lkz/dot_general | solution.py:20
  675.4 28.7 %fusion.15 = f32[64,64,1024]{2,0,1:T(8,128)} fusion(f32[64,64,1024]{2,0,1:T(8,128)} %fusion.9, f32[64,64,1024]{2,0,1:T(8,128)} %get-tuple-element.22), kind=kOutput, calls=%fused_computation.37 | convolution fusion | flops 1614864384 | bytes 50331648 | tf_op jit(solution)/shard_map/lc,kcz->lkz/dot_general | solution.py:20
  704.2 17.9 %copy.169 = f32[64,64,1024]{2,1,0:T(8,128)} copy(f32[64,64,1024]{2,0,1:T(8,128)} %fusion.15) | data formatting | bytes 33554432 | tf_op jit(solution)/shard_map/add | solution.py:46
  722.1 20.4 %stack.27 = f32[1,8,512,4,256]{4,3,2,1,0:T(4,128)} reshape(f32[64,64,1024]{2,1,0:T(8,128)} %copy.169) | data formatting | bytes 33554432 | tf_op jit(solution)/shard_map/stack | solution.py:53
  742.5 14.1 copy.173
  756.6 29.0 %fusion.18 = f32[64,64,1024]{2,0,1:T(8,128)} fusion(f32[64,64,1024]{2,0,1:T(8,128)} %fusion.7, f32[64,64,1024]{2,0,1:T(8,128)} %get-tuple-element.22), kind=kOutput, calls=%fused_computation.38 | convolution fusion | flops 1614864384 | bytes 50331648 | tf_op jit(solution)/shard_map/lc,kcz->lkz/dot_general | solution.py:20
  785.5 17.9 %copy.172 = f32[64,64,1024]{2,1,0:T(8,128)} copy(f32[64,64,1024]{2,0,1:T(8,128)} %fusion.18) | data formatting | bytes 33554432 | tf_op jit(solution)/shard_map/sub | solution.py:49
  803.4 20.4 %stack.28 = f32[1,8,512,4,256]{4,3,2,1,0:T(4,128)} reshape(f32[64,64,1024]{2,1,0:T(8,128)} %copy.172) | data formatting | bytes 33554432 | tf_op jit(solution)/shard_map/stack | solution.py:53
  823.7 9.4 copy.174
  833.2 9.2 fusion
  842.3 6.4 fusion.142
  848.7 8.2 gather_fusion.2
  856.9 8.2 gather_fusion.3
  865.1 7.8 pad_maximum_fusion
  872.8 2.6 copy.175
  875.4 8.2 bitcast_select_fusion
  883.6 22.1 %copy.176 = bf16[2,4096,4,256]{3,2,0,1:T(4,128)(2,1)} copy(bf16[2,4096,4,256]{3,1,2,0:T(8,128)(2,1)} %bitcast_select_fusion) | data formatting | bytes 33554432 | tf_op jit(solution)/shard_map/jit(_take)/select_n | solution.py:65
  905.8 5.9 all-to-all-start.1
  912.1 5.7 gather_fusion
  917.8 5.5 gather_fusion.1
  923.4 1.7 slice_reduce_fusion.1
  925.7 2.4 fusion.144
  928.1 0.6 fusion.145
  928.8 17.0 %multiply_cosine_fusion = (f32[512,2048]{0,1:T(8,128)}, f32[512,2048]{0,1:T(8,128)}) fusion(f32[2048]{0:T(1024)S(1)} %copy-done.12, f32[512]{0:T(512)S(1)} %dynamic-slice_convert_fusion), kind=kLoop, calls=%fused_computation.48 | loop fusion | flops 1048576 | bytes 8398848 | tf_op jit(solution)/shard_map/cos | solution.py:73
  945.7 10.4 fusion.35
  956.2 8.1 fusion.47
  964.3 309.4 %all-to-all-done.1 = bf16[2,4096,4,256]{3,2,0,1:T(4,128)(2,1)} async-done(((bf16[2,4096,4,256]{3,2,0,1:T(4,128)(2,1)}), bf16[2,4096,4,256]{3,2,0,1:T(4,128)(2,1)}, u32[]{:S(2)}, u32[]{:S(2)}) %all-to-all-start.1) | async-done | bytes 16777248 | tf_op jit(solution)/shard_map/all_to_all | solution.py:121
  1273.7 10.0 copy.177
  1283.7 11.2 convert_bitcast_fusion
  1294.9 21.7 %fusion.141 = (f32[1,512,4,8,256]{4,1,3,2,0:T(8,128)}, f32[1,512,4,8,256]{4,1,3,2,0:T(8,128)}) fusion(f32[2,512,4,8,256]{4,1,3,2,0:T(8,128)} %convert_bitcast_fusion), kind=kLoop, calls=%fused_computation.188 | loop fusion | bytes 67108864 | tf_op jit(solution)/shard_map/slice | solution.py:76
  1316.6 16.3 copy.178
  1333.0 16.4 copy.179
  1349.3 24.4 %multiply_add_fusion = (f32[512,4,2048]{0,2,1:T(8,128)}, f32[512,4,2048]{0,2,1:T(8,128)}) fusion(f32[512,4,2048]{0,2,1:T(8,128)} %bitcast.149, f32[512,4,2048]{0,2,1:T(8,128)} %bitcast.148, f32[512,2048]{0,1:T(8,128)} %get-tuple-element.45, f32[512,2048]{0,1:T(8,128)} %get-tuple-element.44), kind=kLoop, calls=%fused_computation.26 | loop fusion | flops 25165824 | bytes 75497472 | tf_op jit(solution)/shard_map/add | solution.py:76
  1373.7 21.8 %fusion.5 = bf16[512,4,2048]{0,2,1:T(8,128)(2,1)} fusion(f32[4,2048,512]{2,1,0:T(8,128)} %fusion.35, f32[512,4,2048]{0,2,1:T(8,128)} %get-tuple-element.20, f32[512,4,2048]{0,2,1:T(8,128)} %get-tuple-element.21, f32[2048]{0:T(1024)S(1)} %get-tuple-element.37, f32[2048]{0:T(1024)S(1)} %get-tuple-element.36, bf16[2,4,2048,256]{3,2,1,0:T(8,128)(2,1)} %param.8, ...), kind=kOutput, calls=%fused_computation.21 | convolution fusion | flops 2172649472 | bytes 63979520 | tf_op jit(solution)/shard_map/mfk,fbk->mfb/dot_general | solution.py:26
  1395.5 8.8 fusion.33
  1404.3 21.9 %fusion.6 = bf16[512,4,2048]{0,2,1:T(8,128)(2,1)} fusion(f32[4,2048,512]{2,1,0:T(8,128)} %fusion.47, f32[512,4,2048]{0,2,1:T(8,128)} %get-tuple-element.21, f32[512,4,2048]{0,2,1:T(8,128)} %get-tuple-element.20, f32[2048]{0:T(1024)S(1)} %get-tuple-element.37, f32[2048]{0:T(1024)S(1)} %get-tuple-element.36, bf16[2,4,2048,256]{3,2,1,0:T(8,128)(2,1)} %param.8, ...), kind=kOutput, calls=%fused_computation.23 | convolution fusion | flops 2172649472 | bytes 63979520 | tf_op jit(solution)/shard_map/mfk,fbk->mfb/dot_general | solution.py:26
  1426.2 9.0 fusion.31
  1435.2 8.3 subtract_convert_fusion
  1443.5 8.1 fusion.29
  1451.6 8.1 fusion.38
  1459.8 8.2 add_convert_fusion
  1468.0 9.4 fusion.40
  1477.4 28.6 %fusion.4 = (f32[2048]{0:T(1024)S(1)}, f32[2048]{0:T(1024)S(1)}) fusion(f32[512,4,2048]{0,2,1:T(8,128)} %get-tuple-element.20, f32[512,4,2048]{0,2,1:T(8,128)} %get-tuple-element.21, f32[4,512,2048]{1,2,0:T(8,128)} %fusion.38, f32[4,512,2048]{1,2,0:T(8,128)} %fusion.40, f32[4,512,2048]{1,2,0:T(8,128)} %fusion.29, bf16[2,4,2048,256]{3,2,1,0:T(8,128)(2,1)} %param.8, ...), kind=kOutput, calls=%fused_computation.17 | convolution fusion | flops 2189422592 | bytes 89145344 | tf_op jit(solution)/shard_map/mfk,fbk->mfb/dot_general | solution.py:26
  1506.1 14.8 scatter_custom_fusion.1
  1520.9 14.8 scatter_custom_fusion.3
  1535.8 14.8 scatter_custom_fusion
  1550.6 14.8 scatter_custom_fusion.2
  1565.4 1.0 copy.199
  1566.7 2.9 copy.190
  1569.6 58.0 %reduce-scatter.4.cloned.1.call-done = f32[128,2]{1,0:T(8,128)} async-done(((f32[1024,2]{1,0:T(8,128)}), f32[128,2]{1,0:T(8,128)}) %reduce-scatter.4.cloned.1.call-update) | async-done | bytes 1040
  1627.7 0.9 copy.200
  1628.6 5.7 psum.7
  (69 shorter events, 3.8 us)
Async XLA Ops:
  44.4 7.8 copy-start.13
  44.4 370.4 %all-to-all-start = ((bf16[2,512,4,2048]{1,2,0,3:T(4,128)(2,1)}), bf16[2,512,4,2048]{1,2,0,3:T(4,128)(2,1)}, u32[]{:S(2)}, u32[]{:S(2)}) async-start(bf16[2,512,4,2048]{1,2,0,3:T(4,128)(2,1)} %copy.159), calls=%async_computation | async-start | bytes 33554432 | tf_op jit(solution)/shard_map/all_to_all | solution.py:119
  52.3 400.0 %copy-start.14 = (s32[8]{0:T(128)}, s32[8]{0:T(128)S(1)}, u32[]{:S(2)}) copy-start(s32[8]{0:T(128)S(1)} %select_reduce_fusion) | copy-start | bytes 100
  872.8 2.6 copy-start.10
  905.8 6.0 copy-start.15
  905.8 6.1 copy-start.11
  905.8 6.3 copy-start.9
  905.8 23.0 %copy-start.12 = (f32[2048]{0:T(1024)S(1)}, f32[2048]{0:T(1024)}, u32[]{:S(2)}) copy-start(f32[2048]{0:T(1024)} %param.11) | copy-start | bytes 24580
  905.8 367.9 %all-to-all-start.1 = ((bf16[2,4096,4,256]{3,2,0,1:T(4,128)(2,1)}), bf16[2,4096,4,256]{3,2,0,1:T(4,128)(2,1)}, u32[]{:S(2)}, u32[]{:S(2)}) async-start(bf16[2,4096,4,256]{3,2,0,1:T(4,128)(2,1)} %copy.176), calls=%async_computation.1 | async-start | bytes 33554432 | tf_op jit(solution)/shard_map/all_to_all | solution.py:121
  911.7 716.0 %reduce-scatter.4.cloned.1.call-start = ((), (), s32[]{:S(2)}) async-start(), calls=%async_computation.3 | async-start | bytes 589824
  925.1 0.6 copy-start.1
  925.1 0.6 copy-start.3
  925.1 3.0 copy-start.5
  925.1 3.6 copy-start.7
  925.7 30.5 %slice-start = ((s8[8388608]{0:T(1024)(128)(4,1)}), s8[4194304]{0:T(1024)(128)(4,1)S(1)}, s32[]{:S(2)}) async-start(s8[8388608]{0:T(1024)(128)(4,1)} %bitcast.142), calls=%async_computation.4 | async-start | bytes 8388608
  945.7 10.5 slice-start.1
  1426.2 17.3 %slice-start.2 = ((s8[8388608]{0:T(1024)(128)(4,1)}), s8[4194304]{0:T(1024)(128)(4,1)S(1)}, s32[]{:S(2)}) async-start(s8[8388608]{0:T(1024)(128)(4,1)} %bitcast.144), calls=%async_computation.6 | async-start | bytes 8388608
  1435.2 8.3 slice-start.3
  1477.4 28.7 %copy-start.2 = (f32[2048]{0:T(1024)S(1)}, f32[2048]{0:T(1024)}, u32[]{:S(2)}) copy-start(f32[2048]{0:T(1024)} %copy-done.1) | copy-start | bytes 24580
  1477.4 28.7 %copy-start.4 = (f32[2048]{0:T(1024)S(1)}, f32[2048]{0:T(1024)}, u32[]{:S(2)}) copy-start(f32[2048]{0:T(1024)} %copy-done.3) | copy-start | bytes 24580
  1477.4 28.7 %copy-start.6 = (f32[2048]{0:T(1024)S(1)}, f32[2048]{0:T(1024)}, u32[]{:S(2)}) copy-start(f32[2048]{0:T(1024)} %copy-done.5) | copy-start | bytes 24580
  1477.4 28.7 %copy-start.8 = (f32[2048]{0:T(1024)S(1)}, f32[2048]{0:T(1024)}, u32[]{:S(2)}) copy-start(f32[2048]{0:T(1024)} %copy-done.7) | copy-start | bytes 24580
  1477.4 89.1 %copy-start = (bf16[4,512,256]{2,1,0:T(8,128)(2,1)S(1)}, bf16[4,512,256]{2,1,0:T(8,128)(2,1)}, u32[]{:S(2)}) copy-start(bf16[4,512,256]{2,1,0:T(8,128)(2,1)} %add_convert_fusion) | copy-start | bytes 3145732
Sparse Core Ops, SparseCore 0:
  1566.6 61.0 reduce-scatter.3
where the time goes:
time: 1650 us; the launch traced here: 1640 us
  waiting for transfers between devices  729 us (44%)
  matrix products  387 us (23%)
  local copies, waits for them, and re-layouts  353 us (21%)
  other arithmetic  139 us (8%)
    all_to_all x1, waiting for transfers between devices, body(): lax.all_to_all(visibilities, 'tm', split_axis=3, concat_axis=1, tiled=True)  361 us
    all_to_all x1, waiting for transfers between devices, body(): lax.all_to_all(ordered, 'tm', split_axis=1, concat_axis=3, tiled=True)  309 us
    dot_general x8, matrix products, table_product(): jnp.einsum(pattern, table, operand, precision=lax.Precision.HIGH, preferr...  236 us
    dot_general x12, matrix products, plain_product(): jnp.einsum(pattern, left_side, right_side, preferred_element_type=jnp.flo...  151 us
    another operation x4, local copies, waits for them, and re-layouts, forward_transform(): jnp.stack([final_real, final_imag]).reshape(2, all_times, columns)  64.2 us
    unnamed x2, waiting for transfers between devices  58 us
    unnamed x49, local copies, waits for them, and re-layouts  46.2 us
    slice x2, local copies, waits for them, and re-layouts, rotate_back(): spectrum[1]  38.1 us
  transfers between devices with their start and end apart: 3, of which 3 were waited for; matrix products, arithmetic and copies ran while one was open for 3% of the time, Pallas kernels for 0%

commit v1 on v0

v1 whole, which is shorter than its diff:
```python
import functools
import math

import jax
import jax.numpy as jnp
from jax import lax
from jax.experimental import pallas as pl
from jax.experimental.pallas import tpu as pltpu
from jax.sharding import PartitionSpec as P

F32 = jnp.float32
BF16 = jnp.bfloat16
RADIX = 4
MIB = 1024 * 1024


def transform_kernel(piece, pieces, chunk, owner_ref, series_ref, beam_ref, gain_ref, table_ref, turn_ref, rot_ref, proj_ref, weight_ref, total_ref):
    tile = pl.program_id(0)
    tile_rows = turn_ref.shape[1]
    width = turn_ref.shape[2]
    modes = beam_ref.shape[2]
    block_rows = proj_ref.shape[1]
    span = pl.num_programs(0) * tile_rows

    @pl.when(tile == 0)
    def _():
        def fill(step, carry):
            rows = pl.ds(pl.multiple_of(step * chunk, chunk), chunk)
            real = beam_ref[0, rows, :].astype(F32)
            imag = beam_ref[1, rows, :].astype(F32)
            for part in range(RADIX):
                gain_real = gain_ref[rows, 2 * part : 2 * part + 1]
                gain_imag = gain_ref[rows, 2 * part + 1 : 2 * part + 2]
                out_real = (real * gain_real + imag * gain_imag).astype(BF16)
                out_imag = (real * gain_imag - imag * gain_real).astype(BF16)
                weight_ref[part, 0, rows, :modes] = out_real
                weight_ref[part, 0, rows, modes:] = out_imag
                weight_ref[part, 1, rows, :modes] = -out_imag
                weight_ref[part, 1, rows, modes:] = out_real
            return carry

        lax.fori_loop(0, width // chunk, fill, 0)

    total_ref[...] = jnp.zeros_like(total_ref)

    def work(step, carry):
        cols = pl.ds(pl.multiple_of(step * chunk, chunk), chunk)
        parts = []
        for part in range(RADIX):
            both = jnp.dot(table_ref[0, part], series_ref[0, part, :, cols], preferred_element_type=F32)
            parts.append((both[:tile_rows], both[tile_rows:]))
        (ar, ai), (br, bi), (cr, ci), (dr, di) = parts
        sr, si, er, ei = ar + cr, ai + ci, ar - cr, ai - ci
        tr, ti, fr, fi = br + dr, bi + di, br - dr, bi - di
        outs = ((sr + tr, si + ti), (er + fi, ei - fr), (sr - tr, si - ti), (er - fi, ei + fr))
        turn_real = turn_ref[0, :, cols].astype(F32)
        turn_imag = turn_ref[1, :, cols].astype(F32)
        for part in range(RADIX):
            xr, xi = outs[part]
            zr = (xr * turn_real - xi * turn_imag).astype(BF16)
            zi = (xr * turn_imag + xi * turn_real).astype(BF16)
            rot_ref[0, part, :, cols] = zr
            rot_ref[1, part, :, cols] = zi
            total_ref[part] += jnp.dot(
                zr, weight_ref[part, 0, cols, :], preferred_element_type=F32
            ) + jnp.dot(zi, weight_ref[part, 1, cols, :], preferred_element_type=F32)
        return carry

    lax.fori_loop(0, width // chunk, work, 0)
    for part in range(RADIX):
        for index in range(pieces):
            row = part * span + tile * tile_rows + index * piece
            owner = owner_ref[row // block_rows]
            start = pl.multiple_of(row % block_rows, piece)
            proj_ref[owner, pl.ds(start, piece), :] = total_ref[
                part, index * piece : (index + 1) * piece, :
            ].astype(BF16)


def transform(owner, series, beam, gains, table, turns, block_rows, tile_rows, channel):
    tiles = table.shape[0]
    width = series.shape[3]
    depth = series.shape[2]
    modes = beam.shape[2]
    span = tiles * tile_rows
    blocks = owner.shape[0]
    piece = min(block_rows, tile_rows)
    chunk = 256
    one = pl.Buffered(1)
    return pl.pallas_call(
        functools.partial(transform_kernel, piece, tile_rows // piece, chunk),
        grid=(tiles,),
        in_specs=[
            pl.BlockSpec(memory_space=pltpu.SMEM),
            pl.BlockSpec((1, RADIX, depth, width), lambda t: (channel, 0, 0, 0), pipeline_mode=one),
            pl.BlockSpec((2, width, modes), lambda t: (0, 0, 0), pipeline_mode=one),
            pl.BlockSpec((width, 2 * RADIX), lambda t: (0, 0), pipeline_mode=one),
            pl.BlockSpec((1, RADIX, 2 * tile_rows, depth), lambda t: (t, 0, 0, 0)),
            pl.BlockSpec((2, tile_rows, width), lambda t: (0, t, 0)),
        ],
        out_specs=[
            pl.BlockSpec((2, RADIX, tile_rows, width), lambda t: (0, 0, t, 0)),
            pl.BlockSpec((blocks, block_rows, 2 * modes), lambda t: (0, 0, 0)),
        ],
        out_shape=[
            jax.ShapeDtypeStruct((2, RADIX, span, width), BF16),
            jax.ShapeDtypeStruct((blocks, block_rows, 2 * modes), BF16),
        ],
        scratch_shapes=[
            pltpu.VMEM((RADIX, 2, width, 2 * modes), BF16),
            pltpu.VMEM((RADIX, tile_rows, 2 * modes), F32),
        ],
        compiler_params=pltpu.CompilerParams(vmem_limit_bytes=62 * MIB),
        cost_estimate=pl.CostEstimate(flops=26 * 10**9, bytes_accessed=60 * MIB, transcendentals=0),
        name="transform",
    )(owner, series, beam, gains, table, turns)


def cross_kernel(owner_ref, grad_ref, rot_ref, beam_ref, gain_ref, out_ref):
    blocks, both, block_rows = grad_ref.shape
    modes = both // 2
    per_part = blocks // RADIX
    sum_real = None
    for part in range(RADIX):
        on_real = on_imag = None
        for index in range(per_part):
            grad = grad_ref[owner_ref[part * per_part + index]]
            rows = slice(index * block_rows, (index + 1) * block_rows)
            new_real = jnp.dot(grad, rot_ref[0, part, rows, :], preferred_element_type=F32)
            new_imag = jnp.dot(grad, rot_ref[1, part, rows, :], preferred_element_type=F32)
            on_real = new_real if on_real is None else on_real + new_real
            on_imag = new_imag if on_imag is None else on_imag + new_imag
        wr = on_real[:modes] + on_imag[modes:]
        wi = on_imag[:modes] - on_real[modes:]
        gain_real = gain_ref[2 * part : 2 * part + 1, :]
        gain_imag = gain_ref[2 * part + 1 : 2 * part + 2, :]
        vr = wr * gain_real - wi * gain_imag
        vi = wr * gain_imag + wi * gain_real
        sum_real, sum_imag = (vr, vi) if sum_real is None else (sum_real + vr, sum_imag + vi)
    br = beam_ref[0].astype(F32)
    bi = beam_ref[1].astype(F32)
    out_ref[0:1, :] = jnp.sum(br * sum_real + bi * sum_imag, axis=0, keepdims=True)
    out_ref[1:2, :] = jnp.sum(br * sum_imag - bi * sum_real, axis=0, keepdims=True)


def cross_terms(owner, grads, rot, beam_turned, gains):
    blocks, both, block_rows = grads.shape
    span, width = rot.shape[2], rot.shape[3]
    modes = both // 2
    chunk = 256
    return pl.pallas_call(
        cross_kernel,
        grid=(width // chunk,),
        in_specs=[
            pl.BlockSpec(memory_space=pltpu.SMEM),
            pl.BlockSpec((blocks, both, block_rows), lambda t: (0, 0, 0)),
            pl.BlockSpec((2, RADIX, span, chunk), lambda t: (0, 0, 0, t)),
            pl.BlockSpec((2, modes, chunk), lambda t: (0, 0, t)),
            pl.BlockSpec((2 * RADIX, chunk), lambda t: (0, t)),
        ],
        out_specs=pl.BlockSpec((2, chunk), lambda t: (0, t)),
        out_shape=jax.ShapeDtypeStruct((2, width), F32),
        compiler_params=pltpu.CompilerParams(vmem_limit_bytes=48 * MIB),
        cost_estimate=pl.CostEstimate(flops=17 * 10**9, bytes_accessed=38 * MIB, transcendentals=0),
        name="cross",
    )(owner, grads, rot, beam_turned, gains)


def times(left, right):
    return (left[0] * right[0] - left[1] * right[1], left[0] * right[1] + left[1] * right[0])


def unit(angle):
    return (jnp.cos(angle), -jnp.sin(angle))


def time_tables(position, slab_rows, all_times, tile_rows):
    span = all_times // RADIX
    fine = 32
    scale = 1.0 / math.sqrt(all_times)
    time_index = position * slab_rows + jnp.arange(slab_rows, dtype=jnp.int32)

    def small(step, count):
        index = step * jnp.arange(count, dtype=jnp.int32)[:, None] * time_index[None, :] % all_times
        return unit(index.astype(F32) * (2.0 * math.pi / all_times))

    coarse_part = small(fine, span // fine)
    fine_part = small(1, fine)
    real, imag = times(
        (coarse_part[0][:, None, :] * scale, coarse_part[1][:, None, :] * scale),
        (fine_part[0][None], fine_part[1][None]),
    )
    tiles = span // tile_rows
    depth = slab_rows // RADIX

    def shaped(value):
        return value.reshape(tiles, tile_rows, depth, RADIX).transpose(0, 3, 1, 2)

    real, imag = shaped(real.astype(BF16)), shaped(imag.astype(BF16))
    top = jnp.concatenate([real, -imag], axis=3)
    bottom = jnp.concatenate([imag, real], axis=3)
    return jnp.concatenate([top, bottom], axis=2)


def phase_tables(rates, span):
    fine = 32
    coarse_index = (fine * jnp.arange(span // fine, dtype=jnp.int32)).astype(F32)
    fine_index = jnp.arange(fine, dtype=jnp.int32).astype(F32)
    coarse_part = unit(coarse_index[:, None] * rates[None, :])
    fine_part = unit(fine_index[:, None] * rates[None, :])
    real, imag = times(
        (coarse_part[0][:, None], coarse_part[1][:, None]), (fine_part[0][None], fine_part[1][None])
    )
    turns = jnp.stack([real.astype(BF16), imag.astype(BF16)]).reshape(2, span, rates.shape[0])
    steps = (span * jnp.arange(RADIX, dtype=jnp.int32)).astype(F32)
    return turns, unit(steps[:, None] * rates[None, :])


def body(visibilities, beam_transfer, sky_modes, inverse_gains, phase_rate, feed_pairs, block_owner):
    devices_tm = lax.axis_size("tm")
    position = lax.axis_index("tm")
    slab_rows, channels, width = visibilities.shape[1:]
    modes = beam_transfer.shape[3]
    all_times = slab_rows * devices_tm
    span = all_times // RADIX
    tile_rows = 256
    depth = slab_rows // RADIX

    series = (
        visibilities.reshape(2, depth, RADIX, channels, width)
        .transpose(3, 2, 0, 1, 4)
        .reshape(channels, RADIX, 2 * depth, width)
    )
    table = time_tables(position, slab_rows, all_times, tile_rows)
    turns, steps = phase_tables(phase_rate, span)
    first_gain = inverse_gains[:, feed_pairs[0]]
    second_gain = inverse_gains[:, feed_pairs[1]]
    pair_real = first_gain[0] * second_gain[0] + first_gain[1] * second_gain[1]
    pair_imag = first_gain[1] * second_gain[0] - first_gain[0] * second_gain[1]
    gained = times(steps, (pair_real[None], pair_imag[None]))
    gains_in = jnp.stack(gained, axis=1).reshape(2 * RADIX, width).T
    gains_out = jnp.stack(steps, axis=1).reshape(2 * RADIX, width)

    beam_real, beam_imag = beam_transfer[0], beam_transfer[1]
    product = functools.partial(jnp.einsum, "fbk,fbl->fkl", preferred_element_type=F32)
    gram_real = product(beam_real, beam_real) + product(beam_imag, beam_imag)
    cross_gram = product(beam_real, beam_imag)
    gram_imag = cross_gram - cross_gram.transpose(0, 2, 1)
    beam_turned = beam_transfer.transpose(1, 0, 3, 2)
    gram = jnp.concatenate(
        [
            jnp.concatenate([gram_real, -gram_imag], axis=2),
            jnp.concatenate([gram_imag, gram_real], axis=2),
        ],
        axis=1,
    )
    gram_high = gram.astype(BF16)
    gram_low = (gram - gram_high.astype(F32)).astype(BF16)

    paired = devices_tm == 8
    slots_out = slots_in = block_owner
    if paired:
        half = devices_tm // 2
        side_slot = (block_owner + position) % 2 * half
        slots_out = side_slot + (block_owner // 2 + half - position // 2) % half
        slots_in = side_slot + block_owner // 2
        lines = [[2 * row + side for row in range(half)] for side in range(2)]
        swap = [(index, index ^ 1) for index in range(devices_tm)]

    def pair_reduce(projected):
        if not paired:
            return lax.psum_scatter(
                projected.reshape(all_times, 2 * modes), "tm", scatter_dimension=0, tiled=True
            )
        other = lax.ppermute(projected[half:], "tm", swap)
        return (projected[:half].astype(F32) + other.astype(F32)).astype(BF16)

    def line_reduce(pair_sum):
        if not paired:
            return pair_sum.astype(F32)
        total = pair_sum[0].astype(F32)
        for shift in range(1, half):
            moves = [(index, (index + 2 * shift) % devices_tm) for index in range(devices_tm)]
            total = total + lax.ppermute(pair_sum[shift], "tm", moves).astype(F32)
        return total

    def gather_blocks(grad_turned):
        if not paired:
            return lax.all_gather(grad_turned, "tm", axis=0)
        near = lax.all_gather(grad_turned, "tm", axis=0, axis_index_groups=lines)
        return jnp.concatenate([near, lax.ppermute(near, "tm", swap)])

    def project(channel, series_all, slots):
        beam = lax.dynamic_index_in_dim(beam_transfer, channel, 1, keepdims=False)
        rot, projected = transform(
            slots, series_all, beam, gains_in, table, turns, slab_rows, tile_rows,
            channel if isinstance(channel, int) else 0,
        )
        return rot, pair_reduce(projected)

    def gradient(channel, mine):
        sky = lax.dynamic_index_in_dim(sky_modes, channel, 2, keepdims=False)
        sky = jnp.concatenate([sky[0], sky[1]], axis=1)
        apply = functools.partial(jnp.einsum, "mk,lk->ml", sky, preferred_element_type=F32)
        mine = line_reduce(mine)
        return (mine - (apply(gram_high[channel]) + apply(gram_low[channel]))).astype(BF16)

    def correlate(channel, rot, grad):
        whole = gather_blocks(grad.T)
        return cross_terms(slots_in, whole, rot, beam_turned[channel], gains_out)

    if devices_tm > 8:

        def step(carry, channel):
            one = lax.dynamic_index_in_dim(series, channel, 0)
            rot, mine = project(channel, one, slots_out)
            grad = gradient(channel, mine)
            cross = correlate(channel, rot, grad)
            return carry + cross, grad

        cross, grads = lax.scan(
            step, jnp.zeros((2, width), F32), jnp.arange(channels, dtype=jnp.int32)
        )
    else:
        rots, grads, waits = [], [], []
        for channel in range(channels):
            now = slots_out
            if channel >= 2:
                now, waits[channel - 2] = lax.optimization_barrier((now, waits[channel - 2]))
            if channel >= 3:
                grad = gradient(channel - 3, waits[channel - 3])
                now, grad = lax.optimization_barrier((now, grad))
                grads.append(grad)
            rot, mine = project(channel, series, now)
            rots.append(rot)
            waits.append(mine)
        for channel in range(len(grads), channels):
            grads.append(gradient(channel, waits[channel]))
        cross = sum(correlate(channel, rots[channel], grads[channel]) for channel in range(channels))
        grads = jnp.stack(grads)
    sky_grad = grads.reshape(channels, slab_rows, 2, modes).transpose(2, 1, 0, 3)

    cross = lax.psum(cross, ("tm", "chan"))
    feed_count = inverse_gains.shape[1]
    share = feed_count // devices_tm
    ids = position * share + jnp.arange(share, dtype=jnp.int32)
    on_first = (feed_pairs[0][:, None] == ids[None, :]).astype(F32)
    on_second = (feed_pairs[1][:, None] == ids[None, :]).astype(F32)
    seconds = jnp.stack(times(first_gain, cross))
    firsts = jnp.stack(times(second_gain, (cross[0], -cross[1])))
    gather = functools.partial(jnp.dot, precision=lax.Precision.HIGHEST)
    feed_grad = gather(seconds, on_second) + gather(firsts, on_first)
    grad_scale = 0.25 / (all_times * channels * lax.axis_size("chan"))
    return (sky_grad, feed_grad * grad_scale)


def solution(mesh):
    placed = (
        P(None, "tm", "chan", None),
        P(None, "chan", None, None),
        P(None, "tm", "chan", None),
        P(),
        P(),
        P(),
        P(),
    )
    return jax.shard_map(
        body,
        mesh=mesh,
        in_specs=placed,
        out_specs=(P(None, "tm", "chan", None), P(None, "tm")),
        check_vma=False,
    )
```

time: 1650 us -> 850 us (0.52)
  waiting for transfers between devices: 729 us -> 150 us
  matrix products: 387 us -> 27.3 us
  Pallas kernels: 0 us -> 337 us
  local copies, waits for them, and re-layouts: 353 us -> 135 us
  other arithmetic: 139 us -> 64.9 us
  blocking collectives: 5.65 us -> 52 us
  starting transfers between devices: 13.3 us -> 58.6 us
    all_to_all x2 -> x0, waiting for transfers between devices: 671 us -> none  [the longest x1 361 us: body(): lax.all_to_all(visibilities, 'tm', split_axis=3, concat_axis=1, tiled=True)]
    dot_general x20 -> x13, matrix products: 387 us -> 27.3 us  [the longest x4 7.84 us: gradient(): apply(gram_low[channel])]
    pallas_call x0 -> x8, Pallas kernels: none -> 337 us  [the longest x4 239 us: transform(): pl.pallas_call(functools.partial(transform_kernel, piece, tile_rows // pi...]
    ppermute x0 -> x20, waiting for transfers between devices: none -> 150 us  [the longest x12 117 us: line_reduce(): total = total + lax.ppermute(pair_sum[shift], 'tm', moves).astype(F32)]
    scatter-add x4 -> x0, other arithmetic: 59.3 us -> none  [the longest x1 14.8 us: feed_terms(): jax.ops.segment_sum(first_real, feed_first, feed_count)]
    ppermute x0 -> x20, starting transfers between devices: none -> 58.5 us  [the longest x12 50.4 us: line_reduce(): total = total + lax.ppermute(pair_sum[shift], 'tm', moves).astype(F32)]
    slice x6 -> x5, local copies, waits for them, and re-layouts: 74.2 us -> 15.9 us  [the longest x4 12.7 us: pair_reduce(): other = lax.ppermute(projected[half:], 'tm', swap)]
    unnamed x2 -> x4, waiting for transfers between devices: 58 us -> 0.07 us
  transfers between devices with their start and end apart: 3 -> 24, of which waited for: 3 -> 10; matrix products, arithmetic and copies ran while one was open for 3% -> 15% of each run, Pallas kernels for 0% -> 30%
where the time goes in v1:
time: 850 us; the launch traced here: 839 us
  Pallas kernels  337 us (40%)
  waiting for transfers between devices  150 us (18%)
  local copies, waits for them, and re-layouts  135 us (16%)
  other arithmetic  64.9 us (8%)
  starting transfers between devices  58.6 us (7%)
  blocking collectives  52 us (6%)
  matrix products  27.3 us (3%)
  between operations  14.8 us (2%)
    pallas_call x4, Pallas kernels, transform(): pl.pallas_call(functools.partial(transform_kernel, piece, tile_rows // pi...  239 us
    ppermute x12, waiting for transfers between devices, line_reduce(): total = total + lax.ppermute(pair_sum[shift], 'tm', moves).astype(F32)  117 us
    pallas_call x4, Pallas kernels, cross_terms(): pl.pallas_call(cross_kernel, grid=(width // chunk,), in_specs=[pl.BlockSp...  97.3 us
    psum x1, blocking collectives, body(): cross = lax.psum(cross, ('tm', 'chan'))  52 us
    ppermute x12, starting transfers between devices, line_reduce(): total = total + lax.ppermute(pair_sum[shift], 'tm', moves).astype(F32)  50.4 us
    ppermute x4, waiting for transfers between devices, gather_blocks(): return jnp.concatenate([near, lax.ppermute(near, 'tm', swap)])  32.6 us
    reshape x1, local copies, waits for them, and re-layouts, body(): visibilities.reshape(2, depth, RADIX, channels, width)  18.6 us
    unnamed x66, local copies, waits for them, and re-layouts  18.3 us
  transfers between devices with their start and end apart: 24, of which 10 were waited for; matrix products, arithmetic and copies ran while one was open for 15% of the time, Pallas kernels for 30%

profile of v1, /device:TPU:0, one launch (start us, length us, event | category | flops | bytes accessed | tf_op | source)
XLA Modules:
  0.0 839.1 jit_solution(16649193136104788540)
XLA Ops:
  9.0 8.6 %add_convert_fusion.1 = (bf16[32,32,512]{1,0,2:T(8,128)(2,1)}, bf16[32,32,512]{1,0,2:T(8,128)(2,1)}) fusion(f32[32,512]{0,1:T(8,128)S(1)} %copy.96, f32[32,512]{0,1:T(8,128)S(1)} %copy.95, f32[32,512]{0,1:T(8,128)S(1)} %copy.94, f32[32,512]{0,1:T(8,128)S(1)} %copy.93), kind=kLoop, calls=%fused_computation.5 | loop fusion | flops 4194304 | bytes 2359296 | tf_op jit(solution)/shard_map/convert_element_type | solution.py:199
  17.6 5.5 convert_element_type.208
  24.3 6.4 convert_element_type.206
  30.6 2.7 copy.97
  33.6 7.6 gather_fusion
  42.8 7.6 gather_fusion.1
  54.4 18.6 %copy.85 = bf16[2,128,4,4,2048]{4,1,0,2,3:T(8,128)(2,1)} copy(bf16[2,128,4,4,2048]{4,3,2,1,0:T(4,128)(2,1)} %bitcast.169) | data formatting | bytes 33554432 | tf_op jit(solution)/shard_map/reshape | solution.py:230
  73.0 5.9 slice_bitcast_fusion.5
  80.9 4.6 subtract_convert_fusion
  85.5 6.3 pad_maximum_fusion.turn_ref
  92.3 3.8 maximum_maximum_fusion.table_ref
  96.1 59.8 %transform.4 = (bf16[2,4,1024,2048]{3,2,1,0:T(8,128)(2,1)}, bf16[8,512,512]{2,1,0:T(8,128)(2,1)}) custom-call(s32[8]{0:T(128)} %fusion.62.owner_ref, bf16[4,4,256,2048]{3,2,1,0:T(8,128)(2,1)} %bitcast.170, bf16[2,2048,256]{2,1,0:T(8,128)(2,1)} %get-tuple-element.41.beam_ref, f32[2048,8]{1,0:T(8,128)} %bitcast.190, ...), custom_call_target="tpu_custom_call" | custom-call | flops 25999998976 | bytes 62914560 | tf_op jit(solution)/shard_map/transform/pallas_call | solution.py:90
  155.9 3.0 slice.211
  159.0 2.9 collective-permute-start
  161.9 59.8 %transform.5 = (bf16[2,4,1024,2048]{3,2,1,0:T(8,128)(2,1)}, bf16[8,512,512]{2,1,0:T(8,128)(2,1)}) custom-call(s32[8]{0:T(128)} %fusion.62.owner_ref, bf16[4,4,256,2048]{3,2,1,0:T(8,128)(2,1)} %bitcast.171, bf16[2,2048,256]{2,1,0:T(8,128)(2,1)} %get-tuple-element.40.beam_ref, f32[2048,8]{1,0:T(8,128)} %bitcast.191, ...), custom_call_target="tpu_custom_call" | custom-call | flops 25999998976 | bytes 62914560 | tf_op jit(solution)/shard_map/transform/pallas_call | solution.py:90
  221.8 3.2 slice.213
  225.0 5.1 fusion
  232.1 5.0 fusion.12
  238.8 3.3 fusion.80
  242.6 2.6 copy-done.13
  249.6 2.6 collective-permute-start.6
  255.5 9.2 %collective-permute-done.5 = bf16[512,512]{1,0:T(8,128)(2,1)S(1)} collective-permute-done((bf16[512,512]{1,0:T(8,128)(2,1)S(1)}, bf16[512,512]{1,0:T(8,128)(2,1)S(1)}, u32[]{:S(2)}, u32[]{:S(2)}) %collective-permute-start.5) | collective-permute-done | bytes 524320 | tf_op jit(solution)/shard_map/ppermute | solution.py:284
  264.6 20.9 %collective-permute-done.6 = bf16[512,512]{1,0:T(8,128)(2,1)S(1)} collective-permute-done((bf16[512,512]{1,0:T(8,128)(2,1)S(1)}, bf16[512,512]{1,0:T(8,128)(2,1)S(1)}, u32[]{:S(2)}, u32[]{:S(2)}) %collective-permute-start.6) | collective-permute-done | bytes 524320 | tf_op jit(solution)/shard_map/ppermute | solution.py:284
  287.0 2.8 add_convert_fusion.4
  292.3 11.7 %collective-permute-start.2 = (bf16[512,512]{1,0:T(8,128)(2,1)}, bf16[512,512]{1,0:T(8,128)(2,1)}, u32[]{:S(2)}, u32[]{:S(2)}) collective-permute-start(bf16[512,512]{1,0:T(8,128)(2,1)} %get-tuple-element.60), channel_id=1, source_target_pairs={{0,8},{4,12},{8,16},{12,20},{16,24},{20,28},{24,0},{28,4},{1,9},{5... | collective-permute-start | bytes 1572872 | tf_op jit(solution)/shard_map/ppermute | solution.py:284
  306.3 59.8 %transform.6 = (bf16[2,4,1024,2048]{3,2,1,0:T(8,128)(2,1)}, bf16[8,512,512]{2,1,0:T(8,128)(2,1)}) custom-call(s32[8]{0:T(128)} %fusion.62.owner_ref, bf16[4,4,256,2048]{3,2,1,0:T(8,128)(2,1)} %bitcast.172, bf16[2,2048,256]{2,1,0:T(8,128)(2,1)} %get-tuple-element.39.beam_ref, f32[2048,8]{1,0:T(8,128)} %bitcast.192, ...), custom_call_target="tpu_custom_call" | custom-call | flops 25999998976 | bytes 62914560 | tf_op jit(solution)/shard_map/transform/pallas_call | solution.py:90
  366.1 3.1 slice.233
  370.7 3.1 fusion.31
  373.9 59.9 %transform.7 = (bf16[2,4,1024,2048]{3,2,1,0:T(8,128)(2,1)}, bf16[8,512,512]{2,1,0:T(8,128)(2,1)}) custom-call(s32[8]{0:T(128)} %fusion.62.owner_ref, bf16[4,4,256,2048]{3,2,1,0:T(8,128)(2,1)} %bitcast.173, bf16[2,2048,256]{2,1,0:T(8,128)(2,1)} %get-tuple-element.42.beam_ref, f32[2048,8]{1,0:T(8,128)} %bitcast.193, ...), custom_call_target="tpu_custom_call" | custom-call | flops 25999998976 | bytes 62914560 | tf_op jit(solution)/shard_map/transform/pallas_call | solution.py:90
  433.7 3.3 slice.243
  440.3 12.6 %collective-permute-start.10 = (bf16[512,512]{1,0:T(8,128)(2,1)S(1)}, bf16[512,512]{1,0:T(8,128)(2,1)S(1)}, u32[]{:S(2)}, u32[]{:S(2)}) collective-permute-start(bf16[512,512]{1,0:T(8,128)(2,1)S(1)} %get-tuple-element.56), channel_id=1, source_target_pairs={{0,16},{4,20},{8,24},{12,28},{16,0},{20,4},{24,8},{28,12},{1,17},{... | collective-permute-start | bytes 1572872 | tf_op jit(solution)/shard_map/ppermute | solution.py:284
  452.9 3.5 collective-permute-start.11
  459.8 17.1 %collective-permute-done.10 = bf16[512,512]{1,0:T(8,128)(2,1)S(1)} collective-permute-done((bf16[512,512]{1,0:T(8,128)(2,1)S(1)}, bf16[512,512]{1,0:T(8,128)(2,1)S(1)}, u32[]{:S(2)}, u32[]{:S(2)}) %collective-permute-start.10) | collective-permute-done | bytes 524320 | tf_op jit(solution)/shard_map/ppermute | solution.py:284
  476.9 13.5 %collective-permute-done.9 = bf16[512,512]{1,0:T(8,128)(2,1)S(1)} collective-permute-done((bf16[512,512]{1,0:T(8,128)(2,1)S(1)}, bf16[512,512]{1,0:T(8,128)(2,1)S(1)}, u32[]{:S(2)}, u32[]{:S(2)}) %collective-permute-start.9) | collective-permute-done | bytes 524320 | tf_op jit(solution)/shard_map/ppermute | solution.py:284
  491.8 2.5 fusion.35
  494.4 2.8 add_convert_fusion.2
  498.4 8.8 %collective-permute-start.13 = (bf16[512,512]{1,0:T(8,128)(2,1)}, bf16[512,512]{1,0:T(8,128)(2,1)}, u32[]{:S(2)}, u32[]{:S(2)}) collective-permute-start(bf16[512,512]{1,0:T(8,128)(2,1)} %get-tuple-element.57), channel_id=1, source_target_pairs={{0,8},{4,12},{8,16},{12,20},{16,24},{20,28},{24,0},{28,4},{1,9},{5... | collective-permute-start | bytes 1572872 | tf_op jit(solution)/shard_map/ppermute | solution.py:284
  509.1 2.9 collective-permute-start.15
  512.0 4.1 copy.129
  518.5 12.1 %collective-permute-done.13 = bf16[512,512]{1,0:T(8,128)(2,1)} collective-permute-done((bf16[512,512]{1,0:T(8,128)(2,1)}, bf16[512,512]{1,0:T(8,128)(2,1)}, u32[]{:S(2)}, u32[]{:S(2)}) %collective-permute-start.13) | collective-permute-done | bytes 524320 | tf_op jit(solution)/shard_map/ppermute | solution.py:284
  530.6 30.6 %collective-permute-done.14 = bf16[512,512]{1,0:T(8,128)(2,1)} collective-permute-done((bf16[512,512]{1,0:T(8,128)(2,1)}, bf16[512,512]{1,0:T(8,128)(2,1)}, u32[]{:S(2)}, u32[]{:S(2)}) %collective-permute-start.14) | collective-permute-done | bytes 524320 | tf_op jit(solution)/shard_map/ppermute | solution.py:284
  561.2 13.7 %collective-permute-done.15 = bf16[512,512]{1,0:T(8,128)(2,1)} collective-permute-done((bf16[512,512]{1,0:T(8,128)(2,1)}, bf16[512,512]{1,0:T(8,128)(2,1)}, u32[]{:S(2)}, u32[]{:S(2)}) %collective-permute-start.15) | collective-permute-done | bytes 524320 | tf_op jit(solution)/shard_map/ppermute | solution.py:284
  575.0 2.6 fusion.19
  577.6 11.6 %copy.127 = bf16[2,4,2048,256]{2,3,0,1:T(8,128)(2,1)} copy(bf16[2,4,2048,256]{3,2,1,0:T(8,128)(2,1)} %param.8) | data formatting | bytes 16777216 | tf_op args[1]
  589.3 5.7 slice_bitcast_fusion.2
  596.9 2.9 copy.123
  599.8 2.8 copy.122
  603.5 2.8 copy.124
  607.3 2.9 copy.125
  610.2 3.9 copy.126
  614.4 7.2 maximum_bitcast_fusion
  621.7 3.9 copy.130
  627.4 4.6 pad_maximum_fusion.2.grad_ref
  632.0 24.4 %cross.5 = f32[2,2048]{1,0:T(2,128)S(1)} custom-call(s32[8]{0:T(128)S(1)} %get-tuple-element.30.owner_ref, bf16[8,512,512]{2,1,0:T(8,128)(2,1)} %pad_maximum_fusion.2.grad_ref, bf16[2,4,1024,2048]{3,2,1,0:T(8,128)(2,1)} %get-tuple-element.27.rot_ref, bf16[2,256,2048]{2,1,0:T(8,128)(2,1)S(1)} %copy-done.2, f32[8,2048]{1,0:T(8,128)S(1)} %reshape.741.gain_ref), custom_call_target="tpu_custom_call" | custom-call | flops 16999999488 | bytes 39845888 | tf_op jit(solution)/shard_map/cross/pallas_call | solution.py:151
  656.3 6.6 collective-permute-done.16
  663.0 3.9 pad_maximum_fusion.1.grad_ref
  666.9 4.2 copy.131
  673.0 24.4 %cross.4 = f32[2,2048]{1,0:T(2,128)S(1)} custom-call(s32[8]{0:T(128)S(1)} %get-tuple-element.30.owner_ref, bf16[8,512,512]{2,1,0:T(8,128)(2,1)} %pad_maximum_fusion.1.grad_ref, bf16[2,4,1024,2048]{3,2,1,0:T(8,128)(2,1)} %get-tuple-element.26.rot_ref, bf16[2,256,2048]{2,1,0:T(8,128)(2,1)S(1)} %copy-done.1, f32[8,2048]{1,0:T(8,128)S(1)} %reshape.741.gain_ref), custom_call_target="tpu_custom_call" | custom-call | flops 16999999488 | bytes 39845888 | tf_op jit(solution)/shard_map/cross/pallas_call | solution.py:151
  697.3 10.6 %collective-permute-done.18 = bf16[4,512,512]{2,1,0:T(8,128)(2,1)} collective-permute-done((bf16[4,512,512]{2,1,0:T(8,128)(2,1)}, bf16[4,512,512]{2,1,0:T(8,128)(2,1)}, u32[]{:S(2)}, u32[]{:S(2)}) %collective-permute-start.18) | collective-permute-done | bytes 2097184 | tf_op jit(solution)/shard_map/ppermute | solution.py:291
  707.9 4.0 pad_maximum_fusion.3.grad_ref
  711.9 24.4 %cross.6 = f32[2,2048]{1,0:T(2,128)S(1)} custom-call(s32[8]{0:T(128)S(1)} %get-tuple-element.30.owner_ref, bf16[8,512,512]{2,1,0:T(8,128)(2,1)} %pad_maximum_fusion.3.grad_ref, bf16[2,4,1024,2048]{3,2,1,0:T(8,128)(2,1)} %get-tuple-element.28.rot_ref, bf16[2,256,2048]{2,1,0:T(8,128)(2,1)S(1)} %copy-done, f32[8,2048]{1,0:T(8,128)S(1)} %reshape.741.gain_ref), custom_call_target="tpu_custom_call" | custom-call | flops 16999999488 | bytes 39845888 | tf_op jit(solution)/shard_map/cross/pallas_call | solution.py:151
  736.3 15.4 %collective-permute-done.19 = bf16[4,512,512]{2,1,0:T(8,128)(2,1)S(1)} collective-permute-done((bf16[4,512,512]{2,1,0:T(8,128)(2,1)}, bf16[4,512,512]{2,1,0:T(8,128)(2,1)S(1)}, u32[]{:S(2)}, u32[]{:S(2)}) %collective-permute-start.19) | collective-permute-done | bytes 2097184 | tf_op jit(solution)/shard_map/ppermute | solution.py:291
  754.1 24.3 %cross.7 = f32[2,2048]{1,0:T(2,128)S(1)} custom-call(s32[8]{0:T(128)S(1)} %get-tuple-element.30.owner_ref, bf16[8,512,512]{2,1,0:T(8,128)(2,1)} %pad_maximum_fusion.4.grad_ref, bf16[2,4,1024,2048]{3,2,1,0:T(8,128)(2,1)} %get-tuple-element.29.rot_ref, bf16[2,256,2048]{2,1,0:T(8,128)(2,1)S(1)} %get-tuple-element.36.beam_ref, f32[8,2048]{1,0:T(8,128)S(1)} %reshape.741.gain_ref), custom_call_target="tpu_custom_call" | custom-call | flops 16999999488 | bytes 39845888 | tf_op jit(solution)/shard_map/cross/pallas_call | solution.py:151
  778.4 52.0 %psum.7 = f32[2,2048]{1,0:T(2,128)S(1)} all-reduce(f32[2,2048]{1,0:T(2,128)S(1)} %add_add_fusion), channel_id=1, replica_groups=mesh['tm'=8,'chan'=4] {'tm','chan'}, use_global_device_ids=true, to_apply=%region_0.1 | all-reduce | flops 4096 | bytes 32768 | tf_op jit(solution)/shard_map/psum | solution.py:343
  (160 shorter events, 56.2 us)
Async XLA Ops:
  7.2 504.9 %all-gather.11.cloned.1.call-start = ((), (), s32[]{:S(2)}) async-start(), calls=%async_computation.1 | async-start | bytes 2621440 | tf_op jit(solution)/shard_map/all_gather | solution.py:290
  24.3 9.0 %copy-start.29 = (f32[2,1024]{1,0:T(2,128)S(1)}, f32[2,1024]{1,0:T(2,128)}, u32[]{:S(2)}) copy-start(f32[2,1024]{1,0:T(2,128)} %param.10) | copy-start | bytes 24580
  24.3 9.3 %copy-start.26 = (s32[2,2048]{1,0:T(2,128)S(1)}, s32[2,2048]{1,0:T(2,128)}, u32[]{:S(2)}) copy-start(s32[2,2048]{1,0:T(2,128)} %param.12) | copy-start | bytes 49156
  24.3 27.7 %copy-start.28 = (f32[2048]{0:T(1024)S(1)}, f32[2048]{0:T(1024)}, u32[]{:S(2)}) copy-start(f32[2048]{0:T(1024)} %param.11) | copy-start | bytes 24580
  42.8 30.3 %copy-start.22 = (f32[2048,2]{0,1:T(2,128)}, f32[2048,2]{0,1:T(2,128)S(1)}, u32[]{:S(2)}) copy-start(f32[2048,2]{0,1:T(2,128)S(1)} %copy.88) | copy-start | bytes 49156
  52.0 21.1 %copy-start.24 = (f32[2048,2]{0,1:T(2,128)}, f32[2048,2]{0,1:T(2,128)S(1)}, u32[]{:S(2)}) copy-start(f32[2048,2]{0,1:T(2,128)S(1)} %copy.90) | copy-start | bytes 49156
  159.0 83.6 %collective-permute-start = (bf16[4,512,512]{2,1,0:T(8,128)(2,1)}, bf16[4,512,512]{2,1,0:T(8,128)(2,1)}, u32[]{:S(2)}, u32[]{:S(2)}) collective-permute-start(bf16[4,512,512]{2,1,0:T(8,128)(2,1)} %slice.211), channel_id=1, source_target_pairs={{0,4},{4,0},{8,12},{12,8},{16,20},{20,16},{24,28},{28,24},{1,5},{5... | collective-permute-start | bytes 6291464 | tf_op jit(solution)/shard_map/ppermute | solution.py:275
  221.8 8.4 slice-start
  225.0 5.2 slice-start.1
  225.0 62.0 %collective-permute-start.1 = (bf16[4,512,512]{2,1,0:T(8,128)(2,1)}, bf16[4,512,512]{2,1,0:T(8,128)(2,1)}, u32[]{:S(2)}, u32[]{:S(2)}) collective-permute-start(bf16[4,512,512]{2,1,0:T(8,128)(2,1)} %slice.213), channel_id=1, source_target_pairs={{0,4},{4,0},{8,12},{12,8},{16,20},{20,16},{24,28},{28,24},{1,5},{5... | collective-permute-start | bytes 6291464 | tf_op jit(solution)/shard_map/ppermute | solution.py:275
  237.2 1.6 copy-start.4
  238.8 46.7 %copy-start.5 = (bf16[4,512,512]{1,2,0:T(8,128)(2,1)}, bf16[4,512,512]{1,2,0:T(8,128)(2,1)S(1)}, u32[]{:S(2)}) copy-start(bf16[4,512,512]{1,2,0:T(8,128)(2,1)S(1)} %subtract_convert_fusion.2) | copy-start | bytes 6291460
  242.1 3.0 copy-start.13
  242.4 11.6 %copy-start.16 = (bf16[4,512,512]{1,2,0:T(8,128)(2,1)}, bf16[4,512,512]{1,2,0:T(8,128)(2,1)S(1)}, u32[]{:S(2)}) copy-start(bf16[4,512,512]{1,2,0:T(8,128)(2,1)S(1)} %fusion.11) | copy-start | bytes 6291460
  242.5 11.5 %copy-start.17 = (bf16[512,256]{1,0:T(8,128)(2,1)}, bf16[512,256]{1,0:T(8,128)(2,1)S(1)}, u32[]{:S(2)}) copy-start(bf16[512,256]{1,0:T(8,128)(2,1)S(1)} %get-tuple-element.102) | copy-start | bytes 786436
  247.4 17.3 %collective-permute-start.5 = (bf16[512,512]{1,0:T(8,128)(2,1)S(1)}, bf16[512,512]{1,0:T(8,128)(2,1)S(1)}, u32[]{:S(2)}, u32[]{:S(2)}) collective-permute-start(bf16[512,512]{1,0:T(8,128)(2,1)S(1)} %get-tuple-element.51), channel_id=1, source_target_pairs={{0,8},{4,12},{8,16},{12,20},{16,24},{20,28},{24,0},{28,4},{1,9},{5... | collective-permute-start | bytes 1572872 | tf_op jit(solution)/shard_map/ppermute | solution.py:284
  249.6 35.9 %collective-permute-start.6 = (bf16[512,512]{1,0:T(8,128)(2,1)S(1)}, bf16[512,512]{1,0:T(8,128)(2,1)S(1)}, u32[]{:S(2)}, u32[]{:S(2)}) collective-permute-start(bf16[512,512]{1,0:T(8,128)(2,1)S(1)} %get-tuple-element.53), channel_id=1, source_target_pairs={{0,16},{4,20},{8,24},{12,28},{16,0},{20,4},{24,8},{28,12},{1,17},{... | collective-permute-start | bytes 1572872 | tf_op jit(solution)/shard_map/ppermute | solution.py:284
  252.2 33.3 %collective-permute-start.7 = (bf16[512,512]{1,0:T(8,128)(2,1)S(1)}, bf16[512,512]{1,0:T(8,128)(2,1)S(1)}, u32[]{:S(2)}, u32[]{:S(2)}) collective-permute-start(bf16[512,512]{1,0:T(8,128)(2,1)S(1)} %get-tuple-element.52), channel_id=1, source_target_pairs={{0,24},{4,28},{8,0},{12,4},{16,8},{20,12},{24,16},{28,20},{1,25},{... | collective-permute-start | bytes 1572872 | tf_op jit(solution)/shard_map/ppermute | solution.py:284
  286.9 323.3 %all-gather.9.cloned.1.call-start = ((), (), s32[]{:S(2)}) async-start(), calls=%async_computation | async-start | bytes 2621440 | tf_op jit(solution)/shard_map/all_gather | solution.py:290
  289.8 1.3 copy-start.3
  292.3 78.4 %collective-permute-start.2 = (bf16[512,512]{1,0:T(8,128)(2,1)}, bf16[512,512]{1,0:T(8,128)(2,1)}, u32[]{:S(2)}, u32[]{:S(2)}) collective-permute-start(bf16[512,512]{1,0:T(8,128)(2,1)} %get-tuple-element.60), channel_id=1, source_target_pairs={{0,8},{4,12},{8,16},{12,20},{16,24},{20,28},{24,0},{28,4},{1,9},{5... | collective-permute-start | bytes 1572872 | tf_op jit(solution)/shard_map/ppermute | solution.py:284
  304.0 66.7 %collective-permute-start.3 = (bf16[512,512]{1,0:T(8,128)(2,1)}, bf16[512,512]{1,0:T(8,128)(2,1)}, u32[]{:S(2)}, u32[]{:S(2)}) collective-permute-start(bf16[512,512]{1,0:T(8,128)(2,1)} %get-tuple-element.62), channel_id=1, source_target_pairs={{0,16},{4,20},{8,24},{12,28},{16,0},{20,4},{24,8},{28,12},{1,17},{... | collective-permute-start | bytes 1572872 | tf_op jit(solution)/shard_map/ppermute | solution.py:284
  305.6 65.1 %collective-permute-start.4 = (bf16[512,512]{1,0:T(8,128)(2,1)}, bf16[512,512]{1,0:T(8,128)(2,1)}, u32[]{:S(2)}, u32[]{:S(2)}) collective-permute-start(bf16[512,512]{1,0:T(8,128)(2,1)} %get-tuple-element.61), channel_id=1, source_target_pairs={{0,24},{4,28},{8,0},{12,4},{16,8},{20,12},{24,16},{28,20},{1,25},{... | collective-permute-start | bytes 1572872 | tf_op jit(solution)/shard_map/ppermute | solution.py:284
  366.1 4.6 copy-start.18
  366.1 4.6 copy-start.20
  369.3 68.6 %collective-permute-start.8 = (bf16[4,512,512]{2,1,0:T(8,128)(2,1)}, bf16[4,512,512]{2,1,0:T(8,128)(2,1)}, u32[]{:S(2)}, u32[]{:S(2)}) collective-permute-start(bf16[4,512,512]{2,1,0:T(8,128)(2,1)} %slice.233), channel_id=1, source_target_pairs={{0,4},{4,0},{8,12},{12,8},{16,20},{20,16},{24,28},{28,24},{1,5},{5... | collective-permute-start | bytes 6291464 | tf_op jit(solution)/shard_map/ppermute | solution.py:275
  373.8 247.8 %all-gather.13.cloned.1.call-start = ((), (), s32[]{:S(2)}) async-start(), calls=%async_computation.2 | async-start | bytes 2621440 | tf_op jit(solution)/shard_map/all_gather | solution.py:290
  433.7 4.2 copy-start.14
  437.0 57.4 %collective-permute-start.12 = (bf16[4,512,512]{2,1,0:T(8,128)(2,1)}, bf16[4,512,512]{2,1,0:T(8,128)(2,1)}, u32[]{:S(2)}, u32[]{:S(2)}) collective-permute-start(bf16[4,512,512]{2,1,0:T(8,128)(2,1)} %slice.243), channel_id=1, source_target_pairs={{0,4},{4,0},{8,12},{12,8},{16,20},{20,16},{24,28},{28,24},{1,5},{5... | collective-permute-start | bytes 6291464 | tf_op jit(solution)/shard_map/ppermute | solution.py:275
  440.3 36.6 %collective-permute-start.10 = (bf16[512,512]{1,0:T(8,128)(2,1)S(1)}, bf16[512,512]{1,0:T(8,128)(2,1)S(1)}, u32[]{:S(2)}, u32[]{:S(2)}) collective-permute-start(bf16[512,512]{1,0:T(8,128)(2,1)S(1)} %get-tuple-element.56), channel_id=1, source_target_pairs={{0,16},{4,20},{8,24},{12,28},{16,0},{20,4},{24,8},{28,12},{1,17},{... | collective-permute-start | bytes 1572872 | tf_op jit(solution)/shard_map/ppermute | solution.py:284
  452.9 24.0 %collective-permute-start.11 = (bf16[512,512]{1,0:T(8,128)(2,1)S(1)}, bf16[512,512]{1,0:T(8,128)(2,1)S(1)}, u32[]{:S(2)}, u32[]{:S(2)}) collective-permute-start(bf16[512,512]{1,0:T(8,128)(2,1)S(1)} %get-tuple-element.55), channel_id=1, source_target_pairs={{0,24},{4,28},{8,0},{12,4},{16,8},{20,12},{24,16},{28,20},{1,25},{... | collective-permute-start | bytes 1572872 | tf_op jit(solution)/shard_map/ppermute | solution.py:284
  456.4 34.1 %collective-permute-start.9 = (bf16[512,512]{1,0:T(8,128)(2,1)S(1)}, bf16[512,512]{1,0:T(8,128)(2,1)S(1)}, u32[]{:S(2)}, u32[]{:S(2)}) collective-permute-start(bf16[512,512]{1,0:T(8,128)(2,1)S(1)} %get-tuple-element.54), channel_id=1, source_target_pairs={{0,8},{4,12},{8,16},{12,20},{16,24},{20,28},{24,0},{28,4},{1,9},{5... | collective-permute-start | bytes 1572872 | tf_op jit(solution)/shard_map/ppermute | solution.py:284
  491.7 175.2 %all-gather.15.cloned.1.call-start = ((), (), s32[]{:S(2)}) async-start(), calls=%async_computation.3 | async-start | bytes 2621440 | tf_op jit(solution)/shard_map/all_gather | solution.py:290
  491.8 5.4 copy-start.19
  498.4 20.1 %copy-start.27 = (s32[2,2048]{1,0:T(2,128)S(1)}, s32[2,2048]{1,0:T(2,128)}, u32[]{:S(2)}) copy-start(s32[2,2048]{1,0:T(2,128)} %param.12) | copy-start | bytes 49156
  498.4 32.2 %collective-permute-start.13 = (bf16[512,512]{1,0:T(8,128)(2,1)}, bf16[512,512]{1,0:T(8,128)(2,1)}, u32[]{:S(2)}, u32[]{:S(2)}) collective-permute-start(bf16[512,512]{1,0:T(8,128)(2,1)} %get-tuple-element.57), channel_id=1, source_target_pairs={{0,8},{4,12},{8,16},{12,20},{16,24},{20,28},{24,0},{28,4},{1,9},{5... | collective-permute-start | bytes 1572872 | tf_op jit(solution)/shard_map/ppermute | solution.py:284
  507.2 54.1 %collective-permute-start.14 = (bf16[512,512]{1,0:T(8,128)(2,1)}, bf16[512,512]{1,0:T(8,128)(2,1)}, u32[]{:S(2)}, u32[]{:S(2)}) collective-permute-start(bf16[512,512]{1,0:T(8,128)(2,1)} %get-tuple-element.59), channel_id=1, source_target_pairs={{0,16},{4,20},{8,24},{12,28},{16,0},{20,4},{24,8},{28,12},{1,17},{... | collective-permute-start | bytes 1572872 | tf_op jit(solution)/shard_map/ppermute | solution.py:284
  509.1 65.9 %collective-permute-start.15 = (bf16[512,512]{1,0:T(8,128)(2,1)}, bf16[512,512]{1,0:T(8,128)(2,1)}, u32[]{:S(2)}, u32[]{:S(2)}) collective-permute-start(bf16[512,512]{1,0:T(8,128)(2,1)} %get-tuple-element.58), channel_id=1, source_target_pairs={{0,24},{4,28},{8,0},{12,4},{16,8},{20,12},{24,16},{28,20},{1,25},{... | collective-permute-start | bytes 1572872 | tf_op jit(solution)/shard_map/ppermute | solution.py:284
  516.1 111.2 %collective-permute-start.17 = (bf16[4,512,512]{2,1,0:T(8,128)(2,1)}, bf16[4,512,512]{2,1,0:T(8,128)(2,1)}, u32[]{:S(2)}, u32[]{:S(2)}) collective-permute-start(bf16[4,512,512]{2,1,0:T(8,128)(2,1)} %bitcast.177), channel_id=1, source_target_pairs={{0,4},{4,0},{8,12},{12,8},{16,20},{20,16},{24,28},{28,24},{1,5},{5... | collective-permute-start | bytes 6291464 | tf_op jit(solution)/shard_map/ppermute | solution.py:291
  577.6 11.6 %copy-start.21 = (f32[4,2,2048]{2,0,1:T(4,128)S(1)}, f32[4,2,2048]{2,0,1:T(4,128)}, u32[]{:S(2)}) copy-start(f32[4,2,2048]{2,0,1:T(4,128)} %get-tuple-element.104) | copy-start | bytes 196612
  589.3 5.8 copy-start.9
  589.3 6.7 copy-start.10
  596.0 6.6 copy-start.11
  596.9 9.5 %copy-start.12 = (bf16[512,512]{1,0:T(8,128)(2,1)S(1)}, bf16[512,512]{1,0:T(8,128)(2,1)}, u32[]{:S(2)}) copy-start(bf16[512,512]{1,0:T(8,128)(2,1)} %fusion.19) | copy-start | bytes 1572868
  607.3 7.1 copy-start.15
  614.1 48.8 %collective-permute-start.16 = (bf16[4,512,512]{2,1,0:T(8,128)(2,1)}, bf16[4,512,512]{2,1,0:T(8,128)(2,1)}, u32[]{:S(2)}, u32[]{:S(2)}) collective-permute-start(bf16[4,512,512]{2,1,0:T(8,128)(2,1)} %bitcast.181), channel_id=1, source_target_pairs={{0,4},{4,0},{8,12},{12,8},{16,20},{20,16},{24,28},{28,24},{1,5},{5... | collective-permute-start | bytes 6291464 | tf_op jit(solution)/shard_map/ppermute | solution.py:291
  625.6 6.4 copy-start.2
  625.6 82.3 %collective-permute-start.18 = (bf16[4,512,512]{2,1,0:T(8,128)(2,1)}, bf16[4,512,512]{2,1,0:T(8,128)(2,1)}, u32[]{:S(2)}, u32[]{:S(2)}) collective-permute-start(bf16[4,512,512]{2,1,0:T(8,128)(2,1)} %bitcast.179), channel_id=1, source_target_pairs={{0,4},{4,0},{8,12},{12,8},{16,20},{20,16},{24,28},{28,24},{1,5},{5... | collective-permute-start | bytes 6291464 | tf_op jit(solution)/shard_map/ppermute | solution.py:291
  632.0 31.0 %copy-start.7 = (bf16[2048,512]{1,0:T(8,128)(2,1)S(1)}, bf16[2048,512]{1,0:T(8,128)(2,1)}, u32[]{:S(2)}) copy-start(bf16[2048,512]{1,0:T(8,128)(2,1)} %copy.126) | copy-start | bytes 6291460
  671.1 80.6 %collective-permute-start.19 = (bf16[4,512,512]{2,1,0:T(8,128)(2,1)}, bf16[4,512,512]{2,1,0:T(8,128)(2,1)S(1)}, u32[]{:S(2)}, u32[]{:S(2)}) collective-permute-start(bf16[4,512,512]{2,1,0:T(8,128)(2,1)} %bitcast.183), channel_id=1, source_target_pairs={{0,4},{4,0},{8,12},{12,8},{16,20},{20,16},{24,28},{28,24},{1,5},{5... | collective-permute-start | bytes 6291464 | tf_op jit(solution)/shard_map/ppermute | solution.py:291
  671.4 1.6 copy-start.1
  673.0 35.0 %copy-start.6 = (bf16[2048,512]{1,0:T(8,128)(2,1)S(1)}, bf16[2048,512]{1,0:T(8,128)(2,1)}, u32[]{:S(2)}) copy-start(bf16[2048,512]{1,0:T(8,128)(2,1)} %copy.130) | copy-start | bytes 6291460
  697.3 14.6 %copy-start = (bf16[2,256,2048]{2,1,0:T(8,128)(2,1)S(1)}, bf16[2,256,2048]{2,1,0:T(8,128)(2,1)}, u32[]{:S(2)}) copy-start(bf16[2,256,2048]{2,1,0:T(8,128)(2,1)} %get-tuple-element.37.beam_ref) | copy-start | bytes 6291460
  711.9 39.8 %copy-start.8 = (bf16[2048,512]{1,0:T(8,128)(2,1)S(1)}, bf16[2048,512]{1,0:T(8,128)(2,1)}, u32[]{:S(2)}) copy-start(bf16[2048,512]{1,0:T(8,128)(2,1)} %copy.131) | copy-start | bytes 6291460
  754.1 76.2 %copy-start.23 = (f32[2048,2]{0,1:T(2,128)S(1)}, f32[2048,2]{0,1:T(2,128)}, u32[]{:S(2)}) copy-start(f32[2048,2]{0,1:T(2,128)} %copy-done.22) | copy-start | bytes 49156
  754.1 76.2 %copy-start.25 = (f32[2048,2]{0,1:T(2,128)S(1)}, f32[2048,2]{0,1:T(2,128)}, u32[]{:S(2)}) copy-start(f32[2048,2]{0,1:T(2,128)} %copy-done.24) | copy-start | bytes 49156
Sparse Core Ops, SparseCore 0:
  287.0 90.7 all-gather.10
  379.4 53.5 all-gather.8
  491.8 85.0 all-gather.12
  578.3 58.5 all-gather.14
